TPU v7x, 256 devices: a whole 4x4x8 slice. The times are simulated.
256 devices in a mesh: blk: 64 (over y_lo, z, x), row: 4 (over y_hi, core).
Axes of the slice: x: 4, y: 4 (y_hi: 2, y_lo: 2; y = y_hi * 2 + y_lo), z: 8, core: 2. Of those that a mesh axis runs over, the one named last changes fastest.
Arguments:
- transmission: float32 [16384, 2, 8192], P(('blk', 'row')), may hold values from -64 to 64, as said below
- assignment: int32 [256], replicated, may hold values from 0 to 255, each once
- pairing: int32 [2, 64], replicated, may hold values from 0 to 2
Outputs:
- rotated: float32 [16384, 2, 8192], P(('blk', 'row'))
Inputs may be any that keep to these rules, and one draw needn't show every extreme that they name: `transmission`: entries are real and imaginary parts of a measured speckle field; columns and rows have differing gains. `assignment`: A permutation of the block numbers.
All inputs are finite; a program needn't handle non-finite values.
Results may differ from a plain program's by a relative error of at most 0.00016.
Values sent between devices are 32-bit elements; how exact they have to be, the bound alone decides.
A program may use at most 128 MiB of HBM per device.

v0:
```python
import jax
import jax.numpy as jnp
from jax import lax
from jax.sharding import PartitionSpec as P

ROWS = 16384
BLOCK = 32
SLOTS = 4
ROUNDS = 2
NS_STEPS = 6


def shifted(block, axis, distance):
    devices = range(lax.axis_size(axis))
    route = [((i - distance) % len(devices), i) for i in devices]
    return lax.ppermute(block, axis, route)


def kernel_rotation(real_part, imag_part):
    kernel = jnp.concatenate(
        [
            jnp.concatenate([real_part, imag_part], axis=1),
            jnp.concatenate([-imag_part, real_part], axis=1),
        ],
        axis=0,
    )
    scale = jnp.sqrt(jnp.sum(kernel * kernel))
    eye = jnp.eye(kernel.shape[0], dtype=jnp.float32)
    upper = kernel / scale
    lower = eye
    for step in range(NS_STEPS):
        middle = 1.5 * eye - 0.5 * jnp.dot(lower, upper, precision=lax.Precision.HIGHEST)
        upper = jnp.dot(upper, middle, precision=lax.Precision.HIGHEST)
        lower = jnp.dot(middle, lower, precision=lax.Precision.HIGHEST)
    return lower * jnp.sqrt(ROWS / scale)


def pair_rotation(gram):
    half = gram.shape[0] // 2
    real_part = gram[:half, :half] + gram[half:, half:]
    imag_part = gram[:half, half:] - gram[half:, :half]
    return kernel_rotation(real_part, imag_part)


def local_gram(joined):
    return jnp.dot(joined.T, joined, precision=lax.Precision.HIGHEST)


def summed_pair(joined):
    gram = lax.psum(local_gram(joined), "row")
    return jnp.dot(joined, pair_rotation(gram), precision=lax.Precision.HIGHEST)


def column_index(held, total_cols):
    parts = jnp.arange(2, dtype=jnp.int32)[None, :, None, None] * total_cols
    starts = held[:, None, :, None] * BLOCK
    within = jnp.arange(BLOCK, dtype=jnp.int32)[None, None, None, :]
    return (parts + starts + within).reshape(-1)


def slot_columns(slots):
    parts = jnp.arange(2, dtype=jnp.int32)[:, None, None] * (SLOTS * BLOCK)
    starts = slots[None, :, None] * BLOCK
    within = jnp.arange(BLOCK, dtype=jnp.int32)[None, None, :]
    return (parts + starts + within).reshape(-1)


def inverse_of(index):
    return (
        jnp.zeros(index.shape, jnp.int32).at[index].set(jnp.arange(index.shape[0], dtype=jnp.int32))
    )


def turn_held(held):
    return jnp.stack(
        [held[:, 0], jnp.roll(held[:, 1], 1), jnp.roll(held[:, 2], -1), held[:, 3]], axis=1
    )


def on_device(transmission, assignment, pairing):
    nblk = lax.axis_size("blk")
    me_blk = lax.axis_index("blk")
    row_part = transmission.shape[0]
    total_cols = transmission.shape[2]
    orders = jnp.array([[0, 1, 2, 3], [0, 2, 1, 3], [0, 3, 1, 2]], dtype=jnp.int32)
    held = assignment.reshape(nblk, SLOTS)
    flat = transmission.reshape(row_part, 2 * total_cols)
    outgoing = jnp.take(flat, column_index(held, total_cols), axis=1)
    blocks = lax.all_to_all(outgoing, "blk", split_axis=1, concat_axis=0, tiled=True)
    owned_rows = blocks.shape[0]
    for rnd in range(ROUNDS):
        pick = pairing[rnd, me_blk]
        order = orders[pick]
        first_cols = slot_columns(order[0:2])
        second_cols = slot_columns(order[2:4])
        first = jnp.take(blocks, first_cols, axis=1)
        second = jnp.take(blocks, second_cols, axis=1)
        new_first = summed_pair(first)
        new_second = summed_pair(second)
        joined = jnp.concatenate([new_first, new_second], axis=1)
        back = inverse_of(jnp.concatenate([first_cols, second_cols]))
        blocks = jnp.take(joined, back, axis=1)
        if rnd < ROUNDS - 1:
            lanes = owned_rows * 2 * BLOCK // 128
            up_cols = slot_columns(jnp.array([1], dtype=jnp.int32))
            down_cols = slot_columns(jnp.array([2], dtype=jnp.int32))
            moved_up = shifted(jnp.take(blocks, up_cols, axis=1).reshape(lanes, 128), "blk", 1)
            moved_down = shifted(jnp.take(blocks, down_cols, axis=1).reshape(lanes, 128), "blk", -1)
            blocks = blocks.at[:, up_cols].set(moved_up.reshape(owned_rows, 2 * BLOCK))
            blocks = blocks.at[:, down_cols].set(moved_down.reshape(owned_rows, 2 * BLOCK))
            held = turn_held(held)
    returned = lax.all_to_all(blocks, "blk", split_axis=0, concat_axis=1, tiled=True)
    placed = column_index(held, total_cols)
    rotated = jnp.take(returned, inverse_of(placed), axis=1)
    return rotated.reshape(row_part, 2, total_cols)


def solution(mesh):
    placed = (P(("blk", "row"), None, None), P(), P())
    return jax.shard_map(
        on_device,
        mesh=mesh,
        in_specs=placed,
        out_specs=P(("blk", "row"), None, None),
        check_vma=False,
    )
```

profile of v0, /device:TPU:6, one launch (start us, length us, event | category | flops | bytes accessed | tf_op | source)
XLA Modules:
  0.0 666.9 jit_solution(6179644993815325899)
XLA Ops:
  10.4 8.4 %copy.43 = f32[64,2,8192]{0,2,1:T(8,128)} copy(f32[64,2,8192]{2,1,0:T(2,128)} %param.14) | data formatting | bytes 8388608 | tf_op args[0]
  18.8 58.2 %gather_fusion = f32[16384,64]{1,0:T(8,128)} fusion(f32[64,16384]{0,1:T(8,128)} %bitcast.203, s32[16384]{0:T(1024)S(1)} %fusion.68), kind=kCustom, calls=%fused_computation.clone | custom fusion | bytes 8454144 | tf_op jit(solution)/shard_map/jit(_take)/gather | solution.py:88
  77.0 13.1 %broadcast_select_fusion.1 = f32[16384,64]{1,0:T(8,128)} fusion(f32[16384,64]{1,0:T(8,128)} %gather_fusion, pred[16384]{0:T(1024)(128)(4,1)S(1)} %compare_and_fusion.1), kind=kLoop, calls=%fused_computation.20 | loop fusion | flops 1048576 | bytes 8404992 | tf_op jit(solution)/shard_map/jit(_take)/select_n | solution.py:88
  90.1 6.8 %copy.44 = f32[64,64,256]{2,0,1:T(8,128)} copy(f32[64,64,256]{0,2,1:T(8,128)} %bitcast.204) | data formatting | bytes 8388608 | tf_op jit(solution)/shard_map/all_to_all | solution.py:89
  96.9 13.3 %all-to-all-start = ((f32[64,64,256]{2,0,1:T(8,128)}), f32[64,64,256]{2,0,1:T(8,128)}, u32[]{:S(2)}, u32[]{:S(2)}) async-start(f32[64,64,256]{2,0,1:T(8,128)} %copy.44), calls=%async_computation | async-start | bytes 8388608 | tf_op jit(solution)/shard_map/all_to_all | solution.py:89
  117.8 87.9 %all-to-all-done = f32[64,64,256]{2,0,1:T(8,128)} async-done(((f32[64,64,256]{2,0,1:T(8,128)}), f32[64,64,256]{2,0,1:T(8,128)}, u32[]{:S(2)}, u32[]{:S(2)}) %all-to-all-start) | async-done | bytes 4194336 | tf_op jit(solution)/shard_map/all_to_all | solution.py:89
  205.7 5.6 copy.45
  211.3 5.6 gather_fusion.2
  216.9 4.4 gather_fusion.1
  221.3 4.9 fusion.10
  231.0 40.0 %all-reduce.7.cloned.1.call-done = (f32[128,128]{1,0:T(8,128)}, f32[128,128]{1,0:T(8,128)}) async-done(((f32[128,128]{1,0:T(8,128)}, f32[128,128]{1,0:T(8,128)}), (f32[128,128]{1,0:T(8,128)}, f32[128,128]{1,0:T(8,128)})) %all-reduce.7.cloned.1.call-update) | async-done | bytes 131088 | tf_op jit(solution)/shard_map/psum | solution.py:50
  281.9 5.1 fusion.8
  292.1 7.8 %gather_fusion.3 = f32[256,4096]{1,0:T(8,128)} fusion(f32[4096,256]{0,1:T(8,128)} %pad_maximum_fusion, s32[1024]{0:T(1024)S(1)} %pad_clamp_fusion.5), kind=kCustom, calls=%fused_computation.2.clone | custom fusion | bytes 8389632 | tf_op jit(solution)/shard_map/jit(_take)/gather | solution.py:102
  299.9 5.2 select_bitcast_fusion.1
  320.7 21.5 %collective-permute-done = f32[2048,128]{1,0:T(8,128)} collective-permute-done((f32[2048,128]{1,0:T(8,128)}, f32[2048,128]{1,0:T(8,128)}, u32[]{:S(2)}, u32[]{:S(2)}) %collective-permute-start) | collective-permute-done | bytes 1048608 | tf_op jit(solution)/shard_map/ppermute | solution.py:16
  352.6 5.3 scatter_fusion
  357.9 5.5 scatter_fusion.1
  363.4 5.6 gather_fusion.7
  369.0 4.4 gather_fusion.6
  373.5 4.9 fusion.2
  381.1 44.9 %all-reduce.5.cloned.1.call-done = (f32[128,128]{1,0:T(8,128)}, f32[128,128]{1,0:T(8,128)}) async-done(((f32[128,128]{1,0:T(8,128)}, f32[128,128]{1,0:T(8,128)}), (f32[128,128]{1,0:T(8,128)}, f32[128,128]{1,0:T(8,128)})) %all-reduce.5.cloned.1.call-update) | async-done | bytes 131088 | tf_op jit(solution)/shard_map/psum | solution.py:50
  436.8 5.3 fusion
  447.3 7.8 %gather_fusion.8 = f32[256,4096]{1,0:T(8,128)} fusion(f32[4096,256]{0,1:T(8,128)} %pad_maximum_fusion.1, s32[1024]{0:T(1024)S(1)} %pad_clamp_fusion), kind=kCustom, calls=%fused_computation.8.clone | custom fusion | bytes 8389632 | tf_op jit(solution)/shard_map/jit(_take)/gather | solution.py:102
  455.1 4.8 select_bitcast_fusion
  459.9 5.6 copy.51
  465.5 10.7 %all-to-all-start.1 = ((f32[64,64,256]{2,1,0:T(8,128)}), f32[64,64,256]{2,1,0:T(8,128)}, u32[]{:S(2)}, u32[]{:S(2)}) async-start(f32[64,64,256]{2,1,0:T(8,128)} %bitcast.206), calls=%async_computation.1 | async-start | bytes 8388608 | tf_op jit(solution)/shard_map/all_to_all | solution.py:112
  476.8 60.3 %scatter_custom_fusion.4 = s32[16384]{0:T(1024)S(1)} fusion(s32[16384]{0:T(1024)S(1)} %bitcast.209, s32[16384]{0:T(1024)S(1)} %iota.215, s32[]{:T(128)} %constant.15.clone.1), kind=kCustom, calls=%fused_computation.148 | custom fusion | bytes 65540 | tf_op jit(solution)/shard_map/scatter | solution.py:70
  537.2 35.8 %all-to-all-done.1 = f32[64,64,256]{2,1,0:T(8,128)} async-done(((f32[64,64,256]{2,1,0:T(8,128)}), f32[64,64,256]{2,1,0:T(8,128)}, u32[]{:S(2)}, u32[]{:S(2)}) %all-to-all-start.1) | async-done | bytes 4194336 | tf_op jit(solution)/shard_map/all_to_all | solution.py:112
  573.0 6.9 %copy.52 = f32[64,64,256]{0,2,1:T(8,128)} copy(f32[64,64,256]{2,0,1:T(8,128)} %bitcast.32) | data formatting | bytes 8388608 | tf_op jit(solution)/shard_map/all_to_all | solution.py:112
  579.9 58.2 %gather_fusion.9 = f32[16384,64]{1,0:T(8,128)} fusion(f32[64,16384]{0,1:T(8,128)} %bitcast.202, s32[16384]{0:T(1024)S(1)} %fusion.69), kind=kCustom, calls=%fused_computation.4.clone | custom fusion | bytes 8454144 | tf_op jit(solution)/shard_map/jit(_take)/gather | solution.py:114
  638.1 13.1 %broadcast_select_fusion = f32[16384,64]{1,0:T(8,128)} fusion(f32[16384,64]{1,0:T(8,128)} %gather_fusion.9, pred[16384]{0:T(1024)(128)(4,1)S(1)} %compare_and_fusion), kind=kLoop, calls=%fused_computation.19 | loop fusion | flops 1048576 | bytes 8404992 | tf_op jit(solution)/shard_map/jit(_take)/select_n | solution.py:114
  651.2 8.6 %copy.53 = f32[64,2,8192]{2,1,0:T(2,128)} copy(f32[64,2,8192]{0,2,1:T(8,128)} %bitcast.205) | data formatting | bytes 8388608 | tf_op jit(solution)/shard_map/reshape | solution.py:115
  (191 shorter events, 69.7 us)
Async XLA Ops:
  96.9 13.4 %copy-start.4 = (s32[2,64]{1,0:T(2,128)S(1)}, s32[2,64]{1,0:T(2,128)}, u32[]{:S(2)}) copy-start(s32[2,64]{1,0:T(2,128)} %param.16) | copy-start | bytes 1540
  96.9 17.8 %copy-start.5 = (s32[3,4]{1,0:T(4,128)S(1)}, s32[3,4]{1,0:T(4,128)}, u32[]{:S(2)}) copy-start(s32[3,4]{1,0:T(4,128)} %constant.22.clone) | copy-start | bytes 148
  96.9 108.8 %all-to-all-start = ((f32[64,64,256]{2,0,1:T(8,128)}), f32[64,64,256]{2,0,1:T(8,128)}, u32[]{:S(2)}, u32[]{:S(2)}) async-start(f32[64,64,256]{2,0,1:T(8,128)} %copy.44), calls=%async_computation | async-start | bytes 8388608 | tf_op jit(solution)/shard_map/all_to_all | solution.py:89
  110.2 160.8 %all-reduce.7.cloned.1.call-start = ((), (), s32[]{:S(2)}) async-start(), calls=%async_computation.3 | async-start | bytes 262144 | tf_op jit(solution)/shard_map/psum | solution.py:50
  228.9 197.0 %all-reduce.5.cloned.1.call-start = ((), (), s32[]{:S(2)}) async-start(), calls=%async_computation.2 | async-start | bytes 262144 | tf_op jit(solution)/shard_map/psum | solution.py:50
  271.0 5.6 copy-start.2
  287.4 2.2 copy-start
  316.6 25.7 %collective-permute-start = (f32[2048,128]{1,0:T(8,128)}, f32[2048,128]{1,0:T(8,128)}, u32[]{:S(2)}, u32[]{:S(2)}) collective-permute-start(f32[2048,128]{1,0:T(8,128)} %reshape.609), channel_id=1, source_target_pairs={{252,0},{0,4},{4,8},{8,12},{12,16},{16,20},{20,24},{24,28},{28,32}... | collective-permute-start | bytes 3145736 | tf_op jit(solution)/shard_map/ppermute | solution.py:16
  320.2 27.5 %collective-permute-start.1 = (f32[2048,128]{1,0:T(8,128)}, f32[2048,128]{1,0:T(8,128)}, u32[]{:S(2)}, u32[]{:S(2)}) collective-permute-start(f32[2048,128]{1,0:T(8,128)} %reshape.611), channel_id=1, source_target_pairs={{4,0},{8,4},{12,8},{16,12},{20,16},{24,20},{28,24},{32,28},{36,32}... | collective-permute-start | bytes 3145736 | tf_op jit(solution)/shard_map/ppermute | solution.py:16
  425.9 5.6 copy-start.3
  442.6 2.2 copy-start.1
  465.5 107.5 %all-to-all-start.1 = ((f32[64,64,256]{2,1,0:T(8,128)}), f32[64,64,256]{2,1,0:T(8,128)}, u32[]{:S(2)}, u32[]{:S(2)}) async-start(f32[64,64,256]{2,1,0:T(8,128)} %bitcast.206), calls=%async_computation.1 | async-start | bytes 8388608 | tf_op jit(solution)/shard_map/all_to_all | solution.py:112
Sparse Core Ops, SparseCore 0:
  229.0 41.9 all-reduce.6
  381.2 44.7 all-reduce.4
where the time goes:
time: 673 us; the launch traced here: 667 us
  local copies, waits for them, and re-layouts  292 us (43%)
  waiting for transfers between devices  233 us (35%)
  other arithmetic  49.8 us (7%)
  matrix products  44.1 us (7%)
  starting transfers between devices  26.1 us (4%)
  between operations  21.6 us (3%)
    all_to_all x1, waiting for transfers between devices, on_device(): lax.all_to_all(outgoing, 'blk', split_axis=1, concat_axis=0, tiled=True)  87.9 us
    psum x2, waiting for transfers between devices, summed_pair(): gram = lax.psum(local_gram(joined), 'row')  84.8 us
    scatter x3, local copies, waits for them, and re-layouts, inverse_of(): jnp.zeros(index.shape, jnp.int32).at[index]  63.5 us
    gather x1, local copies, waits for them, and re-layouts, on_device(): outgoing = jnp.take(flat, column_index(held, total_cols), axis=1)  58.2 us
    gather x1, local copies, waits for them, and re-layouts, on_device(): rotated = jnp.take(returned, inverse_of(placed), axis=1)  58.2 us
    all_to_all x1, waiting for transfers between devices, on_device(): lax.all_to_all(blocks, 'blk', split_axis=0, concat_axis=1, tiled=True)  35.8 us
    ppermute x2, waiting for transfers between devices, shifted(): return lax.ppermute(block, axis, route)  24.8 us
    gather x2, local copies, waits for them, and re-layouts, on_device(): blocks = jnp.take(joined, back, axis=1)  15.6 us
  transfers between devices with their start and end apart: 6, of which 6 were waited for; matrix products, arithmetic and copies ran while one was open for 11% of the time, Pallas kernels for 0%

commit v1 on v0

--- a/solution.py
+++ b/solution.py
@@ -86,7 +86,10 @@
     held = assignment.reshape(nblk, SLOTS)
     flat = transmission.reshape(row_part, 2 * total_cols)
     outgoing = jnp.take(flat, column_index(held, total_cols), axis=1)
-    blocks = lax.all_to_all(outgoing, "blk", split_axis=1, concat_axis=0, tiled=True)
+    blocks = jnp.concatenate(
+        lax.all_to_all(jnp.stack(jnp.split(outgoing, lax.axis_size("blk"), axis=1)), "blk", 0, 0),
+        axis=0,
+    )
     owned_rows = blocks.shape[0]
     for rnd in range(ROUNDS):
         pick = pairing[rnd, me_blk]

time: 673 us -> 717 us (1.065)
  local copies, waits for them, and re-layouts: 292 us -> 333 us
    unnamed x15 -> x70, local copies, waits for them, and re-layouts: 8.42 us -> 50.2 us
    all_to_all x2 -> x0, local copies, waits for them, and re-layouts: 12.4 us -> none  [on_device(): lax.all_to_all(outgoing, 'blk', split_axis=1, concat_axis=0, tiled=True)]
    another operation x0 -> x2, local copies, waits for them, and re-layouts: none -> 7.48 us  [on_device(): jnp.stack(jnp.split(outgoing, lax.axis_size('blk'), axis=1))]
  transfers between devices with their start and end apart: 6 -> 6, of which waited for: 6 -> 6; matrix products, arithmetic and copies ran while one was open for 11% -> 10% of each run, Pallas kernels for 0% -> 0%
where the time goes in v1:
time: 717 us; the launch traced here: 710 us
  local copies, waits for them, and re-layouts  333 us (46%)
  waiting for transfers between devices  233 us (32%)
  other arithmetic  52.4 us (7%)
  matrix products  44 us (6%)
  starting transfers between devices  26 us (4%)
  between operations  21.5 us (3%)
    all_to_all x1, waiting for transfers between devices, on_device(): lax.all_to_all(jnp.stack(jnp.split(outgoing, lax.axis_size('blk'), axis=1...  88 us
    psum x2, waiting for transfers between devices, summed_pair(): gram = lax.psum(local_gram(joined), 'row')  84.6 us
    scatter x3, local copies, waits for them, and re-layouts, inverse_of(): jnp.zeros(index.shape, jnp.int32).at[index]  63.5 us
    gather x1, local copies, waits for them, and re-layouts, on_device(): outgoing = jnp.take(flat, column_index(held, total_cols), axis=1)  58.2 us
    gather x1, local copies, waits for them, and re-layouts, on_device(): rotated = jnp.take(returned, inverse_of(placed), axis=1)  58.2 us
    unnamed x70, local copies, waits for them, and re-layouts  50.2 us
    all_to_all x1, waiting for transfers between devices, on_device(): lax.all_to_all(blocks, 'blk', split_axis=0, concat_axis=1, tiled=True)  35.8 us
    ppermute x2, waiting for transfers between devices, shifted(): return lax.ppermute(block, axis, route)  24.8 us
  transfers between devices with their start and end apart: 6, of which 6 were waited for; matrix products, arithmetic and copies ran while one was open for 10% of the time, Pallas kernels for 0%

profile of v1, /device:TPU:6, one launch (start us, length us, event | category | flops | bytes accessed | tf_op | source)
XLA Modules:
  0.0 710.3 jit_solution(7517884165174291741)
XLA Ops:
  10.5 8.4 %copy.42 = f32[64,2,8192]{0,2,1:T(8,128)} copy(f32[64,2,8192]{2,1,0:T(2,128)} %param.14) | data formatting | bytes 8388608 | tf_op args[0]
  18.9 58.2 %gather_fusion = f32[16384,64]{1,0:T(8,128)} fusion(f32[64,16384]{0,1:T(8,128)} %bitcast.456, s32[16384]{0:T(1024)S(1)} %fusion.68), kind=kCustom, calls=%fused_computation.clone | custom fusion | bytes 8454144 | tf_op jit(solution)/shard_map/jit(_take)/gather | solution.py:88
  77.0 11.8 %select_bitcast_fusion = f32[64,16384]{0,1:T(8,128)S(1)} fusion(f32[16384,64]{1,0:T(8,128)} %gather_fusion, pred[16384]{0:T(1024)(128)(4,1)S(1)} %compare_and_fusion.1), kind=kLoop, calls=%fused_computation.15 | loop fusion | flops 1048576 | bytes 8404992 | tf_op jit(solution)/shard_map/jit(_take)/select_n | solution.py:88
  131.3 6.8 copy.43
  138.1 13.2 %all-to-all-start = ((f32[64,64,256]{2,1,0:T(8,128)}), f32[64,64,256]{2,1,0:T(8,128)}, u32[]{:S(2)}, u32[]{:S(2)}) async-start(f32[64,64,256]{2,1,0:T(8,128)} %copy.43), calls=%async_computation | async-start | bytes 8388608 | tf_op jit(solution)/shard_map/all_to_all | solution.py:90
  158.8 88.0 %all-to-all-done = f32[64,64,256]{2,1,0:T(8,128)} async-done(((f32[64,64,256]{2,1,0:T(8,128)}), f32[64,64,256]{2,1,0:T(8,128)}, u32[]{:S(2)}, u32[]{:S(2)}) %all-to-all-start) | async-done | bytes 4194336 | tf_op jit(solution)/shard_map/all_to_all | solution.py:90
  246.8 5.6 copy.44
  252.4 5.6 gather_fusion.1
  258.0 4.4 gather_fusion.2
  262.5 4.9 fusion.14
  272.2 40.0 %all-reduce.7.cloned.1.call-done = (f32[128,128]{1,0:T(8,128)}, f32[128,128]{1,0:T(8,128)}) async-done(((f32[128,128]{1,0:T(8,128)}, f32[128,128]{1,0:T(8,128)}), (f32[128,128]{1,0:T(8,128)}, f32[128,128]{1,0:T(8,128)})) %all-reduce.7.cloned.1.call-update) | async-done | bytes 131088 | tf_op jit(solution)/shard_map/psum | solution.py:50
  323.8 5.1 fusion.12
  335.6 7.8 %gather_fusion.3 = f32[256,4096]{1,0:T(8,128)} fusion(f32[4096,256]{0,1:T(8,128)} %pad_maximum_fusion, s32[1024]{0:T(1024)S(1)} %pad_clamp_fusion.5), kind=kCustom, calls=%fused_computation.2.clone | custom fusion | bytes 8389632 | tf_op jit(solution)/shard_map/jit(_take)/gather | solution.py:105
  343.4 5.2 select_bitcast_fusion.2
  362.0 17.9 %collective-permute-done = f32[2048,128]{1,0:T(8,128)} collective-permute-done((f32[2048,128]{1,0:T(8,128)}, f32[2048,128]{1,0:T(8,128)}, u32[]{:S(2)}, u32[]{:S(2)}) %collective-permute-start) | collective-permute-done | bytes 1048608 | tf_op jit(solution)/shard_map/ppermute | solution.py:16
  382.1 6.9 collective-permute-done.1
  393.9 5.3 scatter_fusion
  399.2 5.5 scatter_fusion.1
  404.7 5.7 gather_fusion.6
  414.8 4.9 fusion.6
  422.4 44.6 %all-reduce.5.cloned.1.call-done = (f32[128,128]{1,0:T(8,128)}, f32[128,128]{1,0:T(8,128)}) async-done(((f32[128,128]{1,0:T(8,128)}, f32[128,128]{1,0:T(8,128)}), (f32[128,128]{1,0:T(8,128)}, f32[128,128]{1,0:T(8,128)})) %all-reduce.5.cloned.1.call-update) | async-done | bytes 131088 | tf_op jit(solution)/shard_map/psum | solution.py:50
  478.7 5.3 fusion.4
  490.7 7.8 %gather_fusion.8 = f32[256,4096]{1,0:T(8,128)} fusion(f32[4096,256]{0,1:T(8,128)} %pad_maximum_fusion.1, s32[1024]{0:T(1024)S(1)} %pad_clamp_fusion), kind=kCustom, calls=%fused_computation.8.clone | custom fusion | bytes 8389632 | tf_op jit(solution)/shard_map/jit(_take)/gather | solution.py:105
  498.5 4.8 select_bitcast_fusion.1
  503.3 5.6 copy.50
  508.9 10.7 %all-to-all-start.1 = ((f32[64,64,256]{2,1,0:T(8,128)}), f32[64,64,256]{2,1,0:T(8,128)}, u32[]{:S(2)}, u32[]{:S(2)}) async-start(f32[64,64,256]{2,1,0:T(8,128)} %bitcast.458), calls=%async_computation.1 | async-start | bytes 8388608 | tf_op jit(solution)/shard_map/all_to_all | solution.py:115
  520.2 60.3 %scatter_custom_fusion.4 = s32[16384]{0:T(1024)S(1)} fusion(s32[16384]{0:T(1024)S(1)} %bitcast.461, s32[16384]{0:T(1024)S(1)} %iota.215, s32[]{:T(128)} %constant.15.clone.1), kind=kCustom, calls=%fused_computation.280 | custom fusion | bytes 65540 | tf_op jit(solution)/shard_map/scatter | solution.py:70
  580.6 35.8 %all-to-all-done.1 = f32[64,64,256]{2,1,0:T(8,128)} async-done(((f32[64,64,256]{2,1,0:T(8,128)}), f32[64,64,256]{2,1,0:T(8,128)}, u32[]{:S(2)}, u32[]{:S(2)}) %all-to-all-start.1) | async-done | bytes 4194336 | tf_op jit(solution)/shard_map/all_to_all | solution.py:115
  616.4 6.9 copy.51
  623.3 58.2 %gather_fusion.9 = f32[16384,64]{1,0:T(8,128)} fusion(f32[64,16384]{0,1:T(8,128)} %bitcast.455, s32[16384]{0:T(1024)S(1)} %fusion.69), kind=kCustom, calls=%fused_computation.4.clone | custom fusion | bytes 8454144 | tf_op jit(solution)/shard_map/jit(_take)/gather | solution.py:117
  681.5 13.1 %broadcast_select_fusion = f32[16384,64]{1,0:T(8,128)} fusion(f32[16384,64]{1,0:T(8,128)} %gather_fusion.9, pred[16384]{0:T(1024)(128)(4,1)S(1)} %compare_and_fusion), kind=kLoop, calls=%fused_computation.20 | loop fusion | flops 1048576 | bytes 8404992 | tf_op jit(solution)/shard_map/jit(_take)/select_n | solution.py:117
  694.6 8.6 %copy.52 = f32[64,2,8192]{2,1,0:T(2,128)} copy(f32[64,2,8192]{0,2,1:T(8,128)} %bitcast.457) | data formatting | bytes 8388608 | tf_op jit(solution)/shard_map/reshape | solution.py:118
  (247 shorter events, 116.0 us)
Async XLA Ops:
  131.3 20.0 %copy-start = (s32[2,64]{1,0:T(2,128)S(1)}, s32[2,64]{1,0:T(2,128)}, u32[]{:S(2)}) copy-start(s32[2,64]{1,0:T(2,128)} %param.16) | copy-start | bytes 1540
  131.3 24.3 %copy-start.1 = (s32[3,4]{1,0:T(4,128)S(1)}, s32[3,4]{1,0:T(4,128)}, u32[]{:S(2)}) copy-start(s32[3,4]{1,0:T(4,128)} %constant.22.clone) | copy-start | bytes 148
  138.1 108.7 %all-to-all-start = ((f32[64,64,256]{2,1,0:T(8,128)}), f32[64,64,256]{2,1,0:T(8,128)}, u32[]{:S(2)}, u32[]{:S(2)}) async-start(f32[64,64,256]{2,1,0:T(8,128)} %copy.43), calls=%async_computation | async-start | bytes 8388608 | tf_op jit(solution)/shard_map/all_to_all | solution.py:90
  151.3 160.9 %all-reduce.7.cloned.1.call-start = ((), (), s32[]{:S(2)}) async-start(), calls=%async_computation.3 | async-start | bytes 262144 | tf_op jit(solution)/shard_map/psum | solution.py:50
  270.0 197.0 %all-reduce.5.cloned.1.call-start = ((), (), s32[]{:S(2)}) async-start(), calls=%async_computation.2 | async-start | bytes 262144 | tf_op jit(solution)/shard_map/psum | solution.py:50
  354.2 25.7 %collective-permute-start = (f32[2048,128]{1,0:T(8,128)}, f32[2048,128]{1,0:T(8,128)}, u32[]{:S(2)}, u32[]{:S(2)}) collective-permute-start(f32[2048,128]{1,0:T(8,128)} %reshape.610), channel_id=1, source_target_pairs={{252,0},{0,4},{4,8},{8,12},{12,16},{16,20},{20,24},{24,28},{28,32}... | collective-permute-start | bytes 3145736 | tf_op jit(solution)/shard_map/ppermute | solution.py:16
  361.4 27.5 %collective-permute-start.1 = (f32[2048,128]{1,0:T(8,128)}, f32[2048,128]{1,0:T(8,128)}, u32[]{:S(2)}, u32[]{:S(2)}) collective-permute-start(f32[2048,128]{1,0:T(8,128)} %reshape.612), channel_id=1, source_target_pairs={{4,0},{8,4},{12,8},{16,12},{20,16},{24,20},{28,24},{32,28},{36,32}... | collective-permute-start | bytes 3145736 | tf_op jit(solution)/shard_map/ppermute | solution.py:16
  508.9 107.5 %all-to-all-start.1 = ((f32[64,64,256]{2,1,0:T(8,128)}), f32[64,64,256]{2,1,0:T(8,128)}, u32[]{:S(2)}, u32[]{:S(2)}) async-start(f32[64,64,256]{2,1,0:T(8,128)} %bitcast.458), calls=%async_computation.1 | async-start | bytes 8388608 | tf_op jit(solution)/shard_map/all_to_all | solution.py:115
Sparse Core Ops, SparseCore 0:
  270.2 41.9 all-reduce.6
  422.5 44.5 all-reduce.4
